TPU v7x, 128 devices: a whole 4x4x4 slice. The times are simulated.
128 devices in a mesh: section: 4 (over z_hi, core), win: 32 (over z_lo, y, x).
Axes of the slice: x: 4, y: 4, z: 4 (z_hi: 2, z_lo: 2; z = z_hi * 2 + z_lo), core: 2. Of those that a mesh axis runs over, the one named last changes fastest.
Arguments:
- latent: bfloat16 [24, 256, 256], P(None, 'win'), may hold values from -6 to 6
- anchors: int32 [64, 2], P('win'), may hold values from 0 to 248, as said below
- in_proj: bfloat16 [256, 1280], replicated, may hold values from -0.375 to 0.375
- pos_embed: bfloat16 [256, 1280], replicated, may hold values from -6 to 6
- section_w1: bfloat16 [4, 1280, 2560], P('section'), may hold values from -0.15625 to 0.15625
- section_w2: bfloat16 [4, 2560, 1280], P('section'), may hold values from -0.125 to 0.125
- section_gain: float32 [4, 1280], P('section'), may hold values from 0.5 to 1.5
- skip_w: bfloat16 [2560, 1280], replicated, may hold values from -0.125 to 0.125
- out_proj: bfloat16 [1280, 256], replicated, may hold values from -0.15625 to 0.15625
Outputs:
- noise_avg: bfloat16 [24, 256, 256], P('section', 'win')
Inputs may be any that keep to these rules, and one draw needn't show every extreme that they name: Column 0 holds the row anchor, column 1 the column anchor; the windows are listed in an order drawn at random. Every column anchor that is a multiple of 8 below 256 appears in exactly 2 windows. Let g be a column anchor divided by 8. For even g, the row anchors of those windows are 0 and 8. For odd g, each row anchor lies anywhere from 0 to 8. Every token is covered by at least one window.
All inputs are finite; a program needn't handle non-finite values.
Results may differ from a plain program's by a relative error of at most 0.014.
Values may be sent and summed in bfloat16 or wider, within the bound.
No kernel may reach another device: no remote copies, remote signals or barrier semaphores. Data moves between devices by JAX's collectives and lax.ppermute only.
A program may use at most 128 MiB of HBM per device.

v0:
```python
import jax
import jax.numpy as jnp
from jax import lax
from jax.sharding import PartitionSpec as P

TILE = 16
MB = 1


def shortened(shard):
    return jax.tree.map(lambda a: a.astype(jnp.bfloat16) if a.dtype == jnp.float32 else a, shard)


def shifted(value, axis, steps):
    count = lax.axis_size(axis)
    leading, last = (max(0, -steps), min(count, count - steps))
    return lax.ppermute(value, axis, [(source, source + steps) for source in range(leading, last)])


def rms_block(values, gain, w_first, w_second):
    factor = lax.rsqrt(jnp.mean(values * values, axis=-1, keepdims=True) + 1e-06)
    normed = (values * factor * gain).astype(jnp.bfloat16)
    hidden = jax.nn.gelu(
        jnp.dot(normed, w_first, preferred_element_type=jnp.float32), approximate=True
    ).astype(jnp.bfloat16)
    return values + jnp.dot(hidden, w_second, preferred_element_type=jnp.float32)


def per_device(
    latent, anchors, in_proj, pos_embed, section_w1, section_w2, section_gain, skip_w, out_proj
):
    section_id = lax.axis_index("section")
    sections = lax.axis_size("section")
    slabs = lax.axis_size("win")
    w_first = section_w1[0]
    w_second = section_w2[0]
    gain = section_gain[0]
    panorama = lax.all_gather(latent, "win", axis=1, tiled=True)
    height, width, feat_dim = panorama.shape
    slab_width = latent.shape[1]
    model_dim = in_proj.shape[1]
    win_count = anchors.shape[0]
    micro_count = win_count // MB
    row_count = MB * TILE * TILE
    offsets = jnp.arange(TILE, dtype=jnp.int32)
    position_term = jnp.tile(pos_embed.astype(jnp.float32), (MB, 1))
    zeros_noise = jnp.zeros((row_count, feat_dim), jnp.bfloat16)
    zeros_act = jnp.zeros((row_count, model_dim), jnp.bfloat16)

    def window_tokens(picked):
        row_index = picked[:, 0:1] + offsets[None, :]
        col_index = (picked[:, 1:2] + offsets[None, :]) % width
        tiles = panorama[row_index[:, :, None], col_index[:, None, :]]
        return tiles.reshape(row_count, feat_dim)

    def first_section(received, skipped, index):
        picked = lax.dynamic_slice_in_dim(anchors, index * MB, MB, 0)
        embedded = (
            jnp.dot(window_tokens(picked), in_proj, preferred_element_type=jnp.float32)
            + position_term
        )
        return (rms_block(embedded, gain, w_first, w_second).astype(jnp.bfloat16), zeros_noise)

    def middle_section(received, skipped, index):
        return (
            rms_block(received.astype(jnp.float32), gain, w_first, w_second).astype(jnp.bfloat16),
            zeros_noise,
        )

    def last_section(received, skipped, index):
        joined = jnp.concatenate([received, skipped], axis=1)
        merged = jnp.dot(joined, skip_w, preferred_element_type=jnp.float32)
        deep = rms_block(merged, gain, w_first, w_second).astype(jnp.bfloat16)
        return (
            deep,
            jnp.dot(deep, out_proj, preferred_element_type=jnp.float32).astype(jnp.bfloat16),
        )

    branches = [first_section] + [middle_section] * (sections - 2) + [last_section]

    def run_section(tick, received, skipped, noises):
        index = jnp.clip(tick - section_id, 0, micro_count - 1)
        produced, noise = lax.switch(section_id, branches, received, skipped, index)
        noises = lax.dynamic_update_index_in_dim(noises, noise, index, 0)
        return (produced, noises)

    ticks = micro_count + sections - 1
    noise_init = jnp.zeros((micro_count, row_count, feat_dim), jnp.bfloat16)

    def advance_direct(tick, carry):
        received, queue, noises = carry
        produced, noises = run_section(tick, received, queue[0], noises)
        received = jax.tree.map(
            lambda part, own: part.astype(own.dtype),
            shifted(shortened(produced), "section", 1),
            produced,
        )
        arrived = jax.tree.map(
            lambda part, own: part.astype(own.dtype),
            shifted(shortened(produced), "section", sections - 1),
            produced,
        )
        queue = jnp.concatenate([queue[1:], arrived[None]], axis=0)
        return (received, queue, noises)

    queue_init = jnp.zeros((sections - 1, row_count, model_dim), jnp.bfloat16)
    noises = lax.fori_loop(0, ticks, advance_direct, (zeros_act, queue_init, noise_init))[2]
    live = (section_id == sections - 1).astype(jnp.float32)
    band = height // sections
    placed = noises.reshape(win_count, TILE, TILE, feat_dim).astype(jnp.float32)
    row_index = anchors[:, 0:1] + offsets[None, :]
    col_index = (anchors[:, 1:2] + offsets[None, :]) % width
    band_high = (row_index // band)[:, :, None]
    band_low = (row_index % band)[:, :, None]
    slab_high = (col_index // slab_width)[:, None, :]
    slab_low = (col_index % slab_width)[:, None, :]
    sums = jnp.zeros((sections, slabs, band, slab_width, feat_dim), jnp.float32)
    sums = sums.at[band_high, slab_high, band_low, slab_low].add(placed)
    counts = jnp.zeros((sections, slabs, band, slab_width), jnp.float32)
    counts = counts.at[band_high, slab_high, band_low, slab_low].add(live)
    totals, covered = (
        lax.psum_scatter(
            sums.reshape(sections * slabs, band, slab_width, feat_dim),
            ("section", "win"),
            scatter_dimension=0,
            tiled=True,
        ),
        lax.psum_scatter(
            counts.reshape(sections * slabs, band, slab_width),
            ("section", "win"),
            scatter_dimension=0,
            tiled=True,
        ),
    )
    return (totals[0] / covered[0][..., None]).astype(jnp.bfloat16)


def solution(mesh):
    placed = (
        P(None, "win", None),
        P("win", None),
        P(),
        P(),
        P("section", None, None),
        P("section", None, None),
        P("section", None),
        P(),
        P(),
    )
    return jax.shard_map(
        per_device, mesh=mesh, in_specs=placed, out_specs=P("section", "win", None), check_vma=False
    )
```

profile of v0, /device:TPU:0, one launch (start us, length us, event | category | flops | bytes accessed | tf_op | source)
XLA Modules:
  0.0 1040.8 jit_solution(2678079577195951345)
XLA Ops:
  10.4 131.5 %all-gather.2.cloned.1.call-done = bf16[24,256,256]{2,1,0:T(8,128)(2,1)} async-done(((bf16[24,8,256]{2,1,0:T(8,128)(2,1)}), bf16[24,256,256]{2,1,0:T(8,128)(2,1)}) %all-gather.2.cloned.1.call-update) | async-done | bytes 3145744 | tf_op jit(solution)/shard_map/all_gather | solution.py:38
  144.1 166.2 %while.20 = (s32[]{:T(128)}, bf16[256,1280]{1,0:T(8,128)(2,1)S(1)}, bf16[3,256,1280]{2,1,0:T(8,128)(2,1)}, bf16[2,256,256]{2,1,0:T(8,128)(2,1)}, s32[]{:T(128)},...) while((s32[]{:T(128)}, bf16[256,1280]{1,0:T(8,128)(2,1)S(1)}, ...), condition=%wide.region_9.10_spmd.clone.clone, body=%wide.region_0.9_spmd.clone.clone.sunk | while | flops 5212798976 | bytes 41701416 | solution.py:107
  144.1 15.8 %conditional.14 = (bf16[1,256,256]{2,1,0:T(8,128)(2,1)S(1)}, bf16[256,1280]{1,0:T(8,128)(2,1)}) conditional(s32[]{:T(128)} %get-tuple-element.683, (s32[]{:T(128)}, s32[2,2]{1,0:T(2,128)S(1)}, s32[16]{0:T(128)S(1)}, s32[16]{0:T(128)S(1)}, bf16[24,256,256]{2,1,0:T(8,128)(2,1)}, /*index=5*/bf16[256,1280]{1,0:T(8,128)(2,1)}, ...), branch_computations={%region_1.2_spmd, %region_3.4_spmd, %region_5.6_spmd, %region_7.8_... | conditional | flops 5211815936 | bytes 29641776
  150.6 9.3 convolution_add_fusion.4
  165.5 9.8 collective-permute-done.1
  177.8 15.8 %conditional.14 = (bf16[1,256,256]{2,1,0:T(8,128)(2,1)S(1)}, bf16[256,1280]{1,0:T(8,128)(2,1)}) conditional(s32[]{:T(128)} %get-tuple-element.683, (s32[]{:T(128)}, s32[2,2]{1,0:T(2,128)S(1)}, s32[16]{0:T(128)S(1)}, s32[16]{0:T(128)S(1)}, bf16[24,256,256]{2,1,0:T(8,128)(2,1)}, /*index=5*/bf16[256,1280]{1,0:T(8,128)(2,1)}, ...), branch_computations={%region_1.2_spmd, %region_3.4_spmd, %region_5.6_spmd, %region_7.8_... | conditional | flops 5211815936 | bytes 29641776
  184.3 9.4 convolution_add_fusion.4
  193.6 7.2 collective-permute-start.1
  211.0 15.8 %conditional.14 = (bf16[1,256,256]{2,1,0:T(8,128)(2,1)S(1)}, bf16[256,1280]{1,0:T(8,128)(2,1)}) conditional(s32[]{:T(128)} %get-tuple-element.683, (s32[]{:T(128)}, s32[2,2]{1,0:T(2,128)S(1)}, s32[16]{0:T(128)S(1)}, s32[16]{0:T(128)S(1)}, bf16[24,256,256]{2,1,0:T(8,128)(2,1)}, /*index=5*/bf16[256,1280]{1,0:T(8,128)(2,1)}, ...), branch_computations={%region_1.2_spmd, %region_3.4_spmd, %region_5.6_spmd, %region_7.8_... | conditional | flops 5211815936 | bytes 29641776
  217.4 9.3 convolution_add_fusion.4
  226.8 7.2 collective-permute-start.1
  237.4 4.1 collective-permute-done.1
  244.1 15.8 %conditional.14 = (bf16[1,256,256]{2,1,0:T(8,128)(2,1)S(1)}, bf16[256,1280]{1,0:T(8,128)(2,1)}) conditional(s32[]{:T(128)} %get-tuple-element.683, (s32[]{:T(128)}, s32[2,2]{1,0:T(2,128)S(1)}, s32[16]{0:T(128)S(1)}, s32[16]{0:T(128)S(1)}, bf16[24,256,256]{2,1,0:T(8,128)(2,1)}, /*index=5*/bf16[256,1280]{1,0:T(8,128)(2,1)}, ...), branch_computations={%region_1.2_spmd, %region_3.4_spmd, %region_5.6_spmd, %region_7.8_... | conditional | flops 5211815936 | bytes 29641776
  250.5 9.4 convolution_add_fusion.4
  259.9 7.2 collective-permute-start.1
  270.5 4.1 collective-permute-done.1
  277.2 15.8 %conditional.14 = (bf16[1,256,256]{2,1,0:T(8,128)(2,1)S(1)}, bf16[256,1280]{1,0:T(8,128)(2,1)}) conditional(s32[]{:T(128)} %get-tuple-element.683, (s32[]{:T(128)}, s32[2,2]{1,0:T(2,128)S(1)}, s32[16]{0:T(128)S(1)}, s32[16]{0:T(128)S(1)}, bf16[24,256,256]{2,1,0:T(8,128)(2,1)}, /*index=5*/bf16[256,1280]{1,0:T(8,128)(2,1)}, ...), branch_computations={%region_1.2_spmd, %region_3.4_spmd, %region_5.6_spmd, %region_7.8_... | conditional | flops 5211815936 | bytes 29641776
  283.6 9.3 convolution_add_fusion.4
  293.0 7.2 collective-permute-start.1
  303.6 4.1 collective-permute-done.1
  314.8 67.5 %scatter_fusion = f32[4,32,6,8,256]{4,3,2,1,0:T(8,128)} fusion(f32[4,32,6,8,256]{4,3,2,1,0:T(8,128)} %broadcast_in_dim.68, s32[512]{0:T(512)S(1)} %copy-done, f32[512,256]{1,0:T(8,128)S(1)} %bitcast_convert_fusion), kind=kCustom, calls=%fused_computation.1 | custom fusion | flops 131072 | bytes 1581056 | tf_op jit(solution)/shard_map/scatter-add | solution.py:118
  382.3 35.2 %scatter_fusion.1 = f32[4,32,6,8]{1,3,2,0:T(8,128)S(1)} fusion(f32[4,32,6,8]{1,3,2,0:T(8,128)S(1)} %broadcast_in_dim.112, s32[512]{0:T(512)S(1)} %copy-done, f32[512]{0:T(512)S(1)} %broadcast.424), kind=kCustom, calls=%fused_computation.2 | custom fusion | flops 512 | bytes 14336 | tf_op jit(solution)/shard_map/scatter-add | solution.py:120
  417.8 70.1 %all-reduce = f32[128,6,8]{2,1,0:T(8,128)S(1)} all-reduce(f32[128,6,8]{2,1,0:T(8,128)S(1)} %bitcast.44), channel_id=3, replica_groups=mesh['section'=4,'win'=32] {'section','win'}, use_global_device_ids=true, to_apply=%region_13.14.clone | all-reduce | flops 6144 | bytes 49152
  488.0 544.5 %reduce-scatter.2.cloned.1.call-done = f32[1,6,8,256]{3,2,1,0:T(8,128)} async-done(((f32[128,6,8,256]{3,2,1,0:T(8,128)}), f32[1,6,8,256]{3,2,1,0:T(8,128)}) %reduce-scatter.2.cloned.1.call-update) | async-done | bytes 49168 | tf_op jit(solution)/shard_map/reduce_scatter | solution.py:122
  (123 shorter events, 80.3 us)
Async XLA Ops:
  6.5 137.6 %copy-start.3 = (s32[2,2]{1,0:T(2,128)S(1)}, s32[2,2]{1,0:T(2,128)}, u32[]{:S(2)}) copy-start(s32[2,2]{1,0:T(2,128)} %param.16) | copy-start | bytes 52
  6.5 137.6 %copy-start.2 = (f32[1,1280]{1,0:T(1,128)S(1)}, f32[1,1280]{1,0:T(1,128)}, u32[]{:S(2)}) copy-start(f32[1,1280]{1,0:T(1,128)} %param.21) | copy-start | bytes 15364
  6.5 135.4 %all-gather.2.cloned.1.call-start = ((), (), s32[]{:S(2)}) async-start(), calls=%async_computation.1 | async-start | bytes 3244032 | tf_op jit(solution)/shard_map/all_gather | solution.py:38
  7.3 1025.2 %reduce-scatter.2.cloned.1.call-start = ((), (), s32[]{:S(2)}) async-start(), calls=%async_computation.2 | async-start | bytes 6340608 | tf_op jit(solution)/shard_map/reduce_scatter | solution.py:122
  159.9 15.3 %collective-permute-start.1 = (bf16[256,1280]{1,0:T(8,128)(2,1)}, bf16[256,1280]{1,0:T(8,128)(2,1)}, u32[]{:S(2)}, u32[]{:S(2)}) collective-permute-start(bf16[256,1280]{1,0:T(8,128)(2,1)} %get-tuple-element.625), channel_id=1, source_target_pairs={{0,96},{1,97},{2,98},{3,99},{4,100},{5,101},{6,102},{7,103},{8,104... | collective-permute-start | bytes 1966088 | tf_op jit(solution)/shard_map/while/body/eval_jaxpr/ppermute | solution.py:17
  162.1 15.7 %collective-permute-start = (bf16[256,1280]{1,0:T(8,128)(2,1)}, bf16[256,1280]{1,0:T(8,128)(2,1)S(1)}, u32[]{:S(2)}, u32[]{:S(2)}) collective-permute-start(bf16[256,1280]{1,0:T(8,128)(2,1)} %get-tuple-element.625), channel_id=1, source_target_pairs={{0,32},{32,64},{64,96},{1,33},{33,65},{65,97},{2,34},{34,66},{66,9... | collective-permute-start | bytes 1966088 | tf_op jit(solution)/shard_map/while/body/eval_jaxpr/ppermute | solution.py:17
  193.6 14.8 %collective-permute-start.1 = (bf16[256,1280]{1,0:T(8,128)(2,1)}, bf16[256,1280]{1,0:T(8,128)(2,1)}, u32[]{:S(2)}, u32[]{:S(2)}) collective-permute-start(bf16[256,1280]{1,0:T(8,128)(2,1)} %get-tuple-element.625), channel_id=1, source_target_pairs={{0,96},{1,97},{2,98},{3,99},{4,100},{5,101},{6,102},{7,103},{8,104... | collective-permute-start | bytes 1966088 | tf_op jit(solution)/shard_map/while/body/eval_jaxpr/ppermute | solution.py:17
  200.9 10.1 collective-permute-start
  226.8 14.8 %collective-permute-start.1 = (bf16[256,1280]{1,0:T(8,128)(2,1)}, bf16[256,1280]{1,0:T(8,128)(2,1)}, u32[]{:S(2)}, u32[]{:S(2)}) collective-permute-start(bf16[256,1280]{1,0:T(8,128)(2,1)} %get-tuple-element.625), channel_id=1, source_target_pairs={{0,96},{1,97},{2,98},{3,99},{4,100},{5,101},{6,102},{7,103},{8,104... | collective-permute-start | bytes 1966088 | tf_op jit(solution)/shard_map/while/body/eval_jaxpr/ppermute | solution.py:17
  234.0 10.1 collective-permute-start
  259.9 14.8 %collective-permute-start.1 = (bf16[256,1280]{1,0:T(8,128)(2,1)}, bf16[256,1280]{1,0:T(8,128)(2,1)}, u32[]{:S(2)}, u32[]{:S(2)}) collective-permute-start(bf16[256,1280]{1,0:T(8,128)(2,1)} %get-tuple-element.625), channel_id=1, source_target_pairs={{0,96},{1,97},{2,98},{3,99},{4,100},{5,101},{6,102},{7,103},{8,104... | collective-permute-start | bytes 1966088 | tf_op jit(solution)/shard_map/while/body/eval_jaxpr/ppermute | solution.py:17
  267.1 10.1 collective-permute-start
  293.0 14.8 %collective-permute-start.1 = (bf16[256,1280]{1,0:T(8,128)(2,1)}, bf16[256,1280]{1,0:T(8,128)(2,1)}, u32[]{:S(2)}, u32[]{:S(2)}) collective-permute-start(bf16[256,1280]{1,0:T(8,128)(2,1)} %get-tuple-element.625), channel_id=1, source_target_pairs={{0,96},{1,97},{2,98},{3,99},{4,100},{5,101},{6,102},{7,103},{8,104... | collective-permute-start | bytes 1966088 | tf_op jit(solution)/shard_map/while/body/eval_jaxpr/ppermute | solution.py:17
  300.2 10.1 collective-permute-start
  311.3 3.5 copy-start
Sparse Core Ops, SparseCore 0:
  8.9 132.9 all-gather.1
  382.4 649.9 reduce-scatter.1
where the time goes:
time: 1040 us
  waiting for transfers between devices  703 us (68%)
  other arithmetic  126 us (12%)
  blocking collectives  70.1 us (7%)
  matrix products  54.3 us (5%)
  starting transfers between devices  37.7 us (4%)
  local copies, waits for them, and re-layouts  35.7 us (3%)
  between operations  13.5 us (1%)
    reduce_scatter x1, waiting for transfers between devices, per_device(): lax.psum_scatter(sums.reshape(sections * slabs, band, slab_width, feat_di...  544 us
    all_gather x1, waiting for transfers between devices, per_device(): panorama = lax.all_gather(latent, 'win', axis=1, tiled=True)  132 us
    unnamed x1, blocking collectives  70.1 us
    scatter-add x1, other arithmetic, per_device(): sums = sums.at[band_high, slab_high, band_low, slab_low].add(placed)  67.5 us
    dot_general x5, matrix products, rms_block(): jnp.dot(hidden, w_second, preferred_element_type=jnp.float32)  46.7 us
    ppermute x10, starting transfers between devices, shifted(): lax.ppermute(value, axis, [(source, source + steps) for source in range(l...  37.6 us
    scatter-add x1, other arithmetic, per_device(): counts = counts.at[band_high, slab_high, band_low, slab_low].add(live)  35.2 us
    ppermute x10, waiting for transfers between devices, shifted(): lax.ppermute(value, axis, [(source, source + steps) for source in range(l...  26.4 us
  transfers between devices with their start and end apart: 12, of which 7 were waited for; matrix products, arithmetic and copies ran while one was open for 6% of the time, Pallas kernels for 0%

commit v1 on v0

v1 whole, which is shorter than its diff:
```python
import functools

import jax
import jax.numpy as jnp
from jax import lax
from jax.experimental import pallas as pl
from jax.experimental.pallas import tpu as pltpu
from jax.sharding import PartitionSpec as P

TILE = 16
STRIDE = 8
HALF = TILE // 2
MIB = 1 << 20
F32 = jnp.float32
BF16 = jnp.bfloat16


def gelu(v):
    return jax.nn.gelu(v, approximate=True)


def normalise(v, gain):
    factor = lax.rsqrt(jnp.mean(v * v, axis=-1, keepdims=True) + 1e-06)
    return (v * factor * gain).astype(BF16)


def embed_rows(lat, inp, pos, anchor, half):
    rows = lat[pl.ds(anchor, TILE)].astype(F32)
    tiles = rows.reshape(TILE * HALF, rows.shape[-1]).astype(BF16)
    place = pos[:, half].astype(F32).reshape(TILE * HALF, pos.shape[-1])
    return jnp.dot(tiles, inp[...], preferred_element_type=F32) + place


def load_kernel(
    chunks, meta, lat_h, inp_h, pos_h, gain_h, w1_h, w2_h, skip_h, outp_h,
    y, lat, inp, pos, gain_ref, w1, w2, skip, outp, norm, acc, sems,
):
    section, half = meta[0], meta[1]
    hidden = w1.shape[1]
    size = hidden // chunks
    small = [(lat_h, lat), (inp_h, inp), (pos_h, pos), (gain_h, gain_ref), (outp_h, outp)]
    copies = [pltpu.make_async_copy(a, b, sems.at[k]) for k, (a, b) in enumerate(small)]
    base = len(small)
    for c in range(chunks):
        cut = pl.ds(c * size, size)
        copies.append(pltpu.make_async_copy(w1_h.at[0, :, cut], w1.at[:, cut], sems.at[base + 2 * c]))
        copies.append(pltpu.make_async_copy(w2_h.at[0, cut, :], w2.at[cut, :], sems.at[base + 2 * c + 1]))
    for copy in copies:
        copy.start()
    last = base + 2 * chunks

    @pl.when(section == 3)
    def _():
        pltpu.make_async_copy(skip_h, skip, sems.at[last]).start()

    for k in range(base):
        copies[k].wait()

    @pl.when(section == 0)
    def _():
        v = embed_rows(lat, inp, pos, 0, half)
        acc[...] = v
        norm[...] = normalise(v, gain_ref[...])

    for c in range(chunks):
        cut = pl.ds(c * size, size)
        copies[base + 2 * c].wait()
        copies[base + 2 * c + 1].wait()

        @pl.when(section == 0)
        def _():
            h = gelu(jnp.dot(norm[...], w1[:, cut], preferred_element_type=F32)).astype(BF16)
            acc[...] += jnp.dot(h, w2[cut, :], preferred_element_type=F32)

    @pl.when(section == 0)
    def _():
        y[...] = acc[...].astype(BF16)

    @pl.when(section == 3)
    def _():
        pltpu.make_async_copy(skip_h, skip, sems.at[last]).wait()


def join_kernel(left, right, out):
    a, b = left[...], right[...]
    first = lax.broadcasted_iota(jnp.int32, a.shape, 0) == 0
    out[...] = jnp.where(first, a + b, jnp.maximum(a, b))


def tick_kernel(roles, names, outs, *refs):
    at = dict(zip(names, refs))
    meta = at["meta"]
    section, parity = meta[0], meta[1]
    norm, acc = at["norm"], at["acc"]
    w1, w2 = at["w1"], at["w2"]
    dim, hidden = w1.shape

    def anchor_of(part):
        if part < 2:
            return part * STRIDE
        top = at["table"][1, meta[2]]
        return top if part == 2 else at["table"][0, meta[2]] - top

    if roles[0] is not None:

        @pl.when(section == 0)
        def _():
            part = roles[0]
            half = parity if part < 2 else 1 - parity
            acc[...] = embed_rows(at["lat"], at["inp"], at["pos"], anchor_of(part), half)

    if roles[1] is not None:

        @pl.when(section == 1)
        def _():
            acc[...] = at["near"][...].astype(F32)

    if roles[2] is not None:

        @pl.when(section == 2)
        def _():
            acc[...] = at["far"][...].astype(F32)

    if roles[3] is not None:

        @pl.when(section == 3)
        def _():
            acc[...] = jnp.dot(
                at["near"][...], at["skip"][:dim, :], preferred_element_type=F32
            ) + jnp.dot(at["first"][...], at["skip"][dim:, :], preferred_element_type=F32)

    first_active = min(s for s in range(4) if roles[s] is not None)
    last_active = max(s for s in range(4) if roles[s] is not None)
    active = (section >= first_active) & (section <= last_active)

    @pl.when(active)
    def _():
        norm[...] = normalise(acc[...], at["gain"][...])
        size = hidden // 2
        for c in range(2):
            cut = pl.ds(c * size, size)
            h = gelu(jnp.dot(norm[...], w1[:, cut], preferred_element_type=F32)).astype(BF16)
            acc[...] += jnp.dot(h, w2[cut, :], preferred_element_type=F32)
        if any(r is not None for r in roles[:3]):
            at["y"][...] = acc[...].astype(BF16)

    if roles[3] is not None:
        part = roles[3]
        totals = at["totals"]

        @pl.when(section == 3)
        def _():
            deep = acc[...].astype(BF16)
            noise = jnp.dot(deep, at["outp"][...], preferred_element_type=F32)
            noise = noise.astype(BF16).astype(F32).reshape(TILE, HALF, noise.shape[-1])
            if part == 0:
                totals[...] = jnp.zeros(totals.shape, F32)
            else:
                totals[...] = at["sums"][...]
            rows = pl.ds(anchor_of(part), TILE)
            totals[rows] = totals[rows] + noise
            if part == 3:
                row = lax.broadcasted_iota(jnp.int32, totals.shape, 0)
                count = jnp.zeros(totals.shape, F32)
                for k in range(4):
                    a = anchor_of(k)
                    count += ((row >= a) & (row < a + TILE)).astype(F32)
                at["final"][...] = (totals[...] / count).astype(BF16)


def per_device(
    latent, anchors, in_proj, pos_embed, section_w1, section_w2, section_gain, skip_w, out_proj
):
    section = lax.axis_index("section")
    slab = lax.axis_index("win")
    sections, slabs = lax.axis_size("section"), lax.axis_size("win")
    height, width, feat = latent.shape
    dim = in_proj.shape[1]
    hidden = section_w1.shape[2]
    tokens = TILE * HALF
    parity = slab % 2
    odd = (slab - 1 + parity) % slabs
    axes = ("section", "win")
    positions = pos_embed.reshape(TILE, 2, HALF, dim)

    def hop(value, *pairs):
        return lax.ppermute(
            value, axes, [(a * slabs + w, b * slabs + w) for a, b in pairs for w in range(slabs)]
        )

    smem = pl.BlockSpec(memory_space=pltpu.SMEM)
    vmem = pl.BlockSpec(memory_space=pltpu.VMEM)
    hbm = pl.BlockSpec(memory_space=pltpu.HBM)

    grid = lax.broadcasted_iota(jnp.int32, (2, slabs), 1)
    mine = anchors[:, 1:2] // STRIDE == grid
    rows = anchors[:, 0:1]
    sums = jnp.sum(jnp.where(mine, rows, 0), axis=0)
    tops = jnp.max(jnp.where(mine, rows, -1), axis=0)
    table = jnp.stack([sums, tops])
    step = 1
    while step < slabs:
        other = lax.ppermute(table, "win", [(w, w ^ step) for w in range(slabs)])
        table = pl.pallas_call(
            join_kernel,
            out_shape=jax.ShapeDtypeStruct(table.shape, table.dtype),
            in_specs=[vmem, vmem],
            out_specs=vmem,
            compiler_params=pltpu.CompilerParams(vmem_limit_bytes=MIB),
        )(table, other)
        step *= 2
    meta = jnp.stack([section, parity, odd]).astype(jnp.int32)

    act = jax.ShapeDtypeStruct((tokens, dim), BF16)
    scratch = [pltpu.VMEM((tokens, dim), BF16), pltpu.VMEM((tokens, dim), F32)]
    chunks = 5
    flops = 4 * tokens * dim * hidden

    def like(a, shape=None):
        return jax.ShapeDtypeStruct(shape or a.shape, a.dtype)

    def held(a, shape=None):
        return pltpu.VMEM(shape or a.shape, a.dtype)

    def pinned(a):
        return pltpu.with_memory_space_constraint(a, pltpu.VMEM)

    y, lat, inp, pos, gain, w1, w2, skip, outp = pl.pallas_call(
        functools.partial(load_kernel, chunks),
        out_shape=[
            act, held(latent), held(in_proj), held(positions), held(section_gain),
            held(section_w1, (dim, hidden)), held(section_w2, (hidden, dim)),
            held(skip_w), held(out_proj),
        ],
        in_specs=[smem] + [hbm] * 8,
        out_specs=[vmem] * 9,
        scratch_shapes=scratch + [pltpu.SemaphoreType.DMA((5 + 2 * chunks + 1,))],
        compiler_params=pltpu.CompilerParams(vmem_limit_bytes=16 * MIB),
        cost_estimate=pl.CostEstimate(flops=flops, bytes_accessed=13 * MIB, transcendentals=0),
    )(
        meta,
        *(
            pltpu.with_memory_space_constraint(a, pltpu.HBM)
            for a in (
                latent, in_proj, positions, section_gain, section_w1, section_w2, skip_w, out_proj
            )
        ),
    )

    lat, inp, pos, gain, w1, w2, skip, outp = map(pinned, (lat, inp, pos, gain, w1, w2, skip, outp))

    def tick(roles, **extra):
        given = dict(
            meta=meta, table=table, gain=gain, w1=w1, w2=w2,
        )
        if roles[0] is not None:
            given.update(lat=lat, inp=inp, pos=pos)
        if roles[3] is not None:
            given.update(skip=skip, outp=outp)
        given.update(extra)
        outs = {}
        if any(r is not None for r in roles[:3]):
            outs["y"] = act
        room = []
        if roles[3] == 3:
            outs["final"] = like(latent)
            room = [pltpu.VMEM(latent.shape, F32)]
        elif roles[3] is not None:
            outs["totals"] = jax.ShapeDtypeStruct(latent.shape, F32)
        names = [*given, *outs, "norm", "acc", *(["totals"] if room else [])]
        results = pl.pallas_call(
            functools.partial(tick_kernel, roles, names, list(outs)),
            out_shape=list(outs.values()),
            in_specs=[smem if k in ("meta", "table") else vmem for k in given],
            out_specs=[vmem] * len(outs),
            scratch_shapes=scratch + room,
            compiler_params=pltpu.CompilerParams(vmem_limit_bytes=16 * MIB),
            cost_estimate=pl.CostEstimate(flops=flops, bytes_accessed=MIB, transcendentals=0),
        )(*given.values())
        return dict(zip(outs, results))

    up, cross = (0, 1), (1, 2)
    near0 = hop(y, (0, 1))
    first0 = hop(y, (0, 3))
    y1 = tick((1, 0, None, None), near=near0)["y"]
    near1 = hop(y1, (0, 1))
    far1 = hop(y1, (1, 2), (0, 3))
    y2 = tick((2, 1, None, None), near=near1)["y"]
    near2 = hop(y2, (0, 1))
    far2 = hop(y2, (1, 2), (0, 3))
    y3 = tick((3, 2, 0, None), near=near2, far=far1)["y"]
    near3 = hop(y3, (0, 1), (2, 3))
    far3 = hop(y3, (1, 2))
    out4 = tick((None, 3, 1, 0), near=near3, far=far2, first=first0)
    near4 = hop(out4["y"], (2, 3))
    far4 = hop(out4["y"], (1, 2))
    first3, _ = lax.optimization_barrier((y3, out4["y"]))
    first3 = hop(first3, (0, 3))
    out5 = tick((None, None, 2, 1), near=near4, far=far3, first=far1, sums=out4["totals"])
    near5 = hop(out5["y"], (2, 3))
    out6 = tick((None, None, 3, 2), near=near5, far=far4, first=far2, sums=out5["totals"])
    near6 = hop(out6["y"], (2, 3))
    final = tick((None, None, None, 3), near=near6, first=first3, sums=out6["totals"])["final"]

    band = height // sections
    parts = [final[s * band : (s + 1) * band] for s in range(sections)]
    sent = [hop(parts[s], (3, s)) for s in range(3)]
    result = parts[3]
    for s in range(3):
        result = jnp.where(section == s, sent[s], result)
    return result


def solution(mesh):
    placed = (
        P(None, "win", None),
        P("win", None),
        P(),
        P(),
        P("section", None, None),
        P("section", None, None),
        P("section", None),
        P(),
        P(),
    )
    return jax.shard_map(
        per_device, mesh=mesh, in_specs=placed, out_specs=P("section", "win", None), check_vma=False
    )
```

time: 1040 us -> 90.8 us (0.09)
  waiting for transfers between devices: 703 us -> 27.5 us
  other arithmetic: 126 us -> 0.97 us
  blocking collectives: 70.1 us -> 0 us
  matrix products: 54.3 us -> 0 us
  local copies, waits for them, and re-layouts: 35.7 us -> 0.01 us
  Pallas kernels: 0 us -> 18.5 us
  between operations: 13.5 us -> 0.3 us
    reduce_scatter x1 -> x0, waiting for transfers between devices: 544 us -> none  [per_device(): lax.psum_scatter(sums.reshape(sections * slabs, band, slab_width, feat_di...]
    all_gather x1 -> x0, waiting for transfers between devices: 132 us -> none  [per_device(): panorama = lax.all_gather(latent, 'win', axis=1, tiled=True)]
    scatter-add x2 -> x0, other arithmetic: 103 us -> none  [the longest x1 67.5 us: per_device(): sums = sums.at[band_high, slab_high, band_low, slab_low].add(placed)]
    unnamed x1 -> x0, blocking collectives: 70.1 us -> none
    dot_general x10 -> x0, matrix products: 54.3 us -> none  [the longest x5 46.7 us: rms_block(): jnp.dot(hidden, w_second, preferred_element_type=jnp.float32)]
    pallas_call x0 -> x13, Pallas kernels: none -> 18.5 us  [the longest x7 11.7 us: tick(): pl.pallas_call(functools.partial(tick_kernel, roles, names, list(outs)),...]
    gather x5 -> x0, local copies, waits for them, and re-layouts: 13.8 us -> none  [window_tokens(): tiles = panorama[row_index[:, :, None], col_index[:, None, :]]]
    concatenate x18 -> x0, other arithmetic: 13.1 us -> none  [the longest x5 12.8 us: advance_direct(): queue = jnp.concatenate([queue[1:], arrived[None]], axis=0)]
  transfers between devices with their start and end apart: 12 -> 21, of which waited for: 7 -> 10; matrix products, arithmetic and copies ran while one was open for 6% -> 0% of each run, Pallas kernels for 0% -> 9%
where the time goes in v1:
time: 90.8 us; the launch traced here: 90.3 us
  starting transfers between devices  42.9 us (47%)
  waiting for transfers between devices  27.5 us (30%)
  Pallas kernels  18.5 us (20%)
  other arithmetic  0.97 us (1%)
    ppermute x16, starting transfers between devices, hop(): lax.ppermute(value, axes, [(a * slabs + w, b * slabs + w) for a, b in pai...  31.3 us
    ppermute x16, waiting for transfers between devices, hop(): lax.ppermute(value, axes, [(a * slabs + w, b * slabs + w) for a, b in pai...  18.2 us
    pallas_call x7, Pallas kernels, tick(): pl.pallas_call(functools.partial(tick_kernel, roles, names, list(outs)),...  11.7 us
    ppermute x5, starting transfers between devices, per_device(): other = lax.ppermute(table, 'win', [(w, w ^ step) for w in range(slabs)])  11.7 us
    ppermute x5, waiting for transfers between devices, per_device(): other = lax.ppermute(table, 'win', [(w, w ^ step) for w in range(slabs)])  9.26 us
    pallas_call x1, Pallas kernels, per_device(): pl.pallas_call(functools.partial(load_kernel, chunks), out_shape=[act, he...  6.82 us
  transfers between devices with their start and end apart: 21, of which 10 were waited for; matrix products, arithmetic and copies ran while one was open for 0% of the time, Pallas kernels for 9%

profile of v1, /device:TPU:0, one launch (start us, length us, event | category | flops | bytes accessed | tf_op | source)
XLA Modules:
  0.0 90.3 jit_solution(4416322962604265207)
XLA Ops:
  0.1 6.8 %shard_map.96 = (bf16[128,1280]{1,0:T(8,128)(2,1)S(1)}, bf16[24,8,256]{2,1,0:T(8,128)(2,1)S(1)}, bf16[256,1280]{1,0:T(8,128)(2,1)S(1)}, bf16[16,2,8,1280]{3,2,1,...) custom-call(s32[3]{0:T(128)S(1)} %pad_add_fusion.1.meta.refs_0_, ...), custom_call_target="tpu_custom_call" | custom-call | flops 1677721600 | bytes 13631488 | tf_op jit(solution)/shard_map/pallas_call | solution.py:228
  6.9 1.3 %collective-permute-start.5 = (bf16[128,1280]{1,0:T(8,128)(2,1)S(1)}, bf16[128,1280]{1,0:T(8,128)(2,1)S(1)}, u32[]{:S(2)}, u32[]{:S(2)}) collective-permute-start(bf16[128,1280]{1,0:T(8,128)(2,1)S(1)} %get-tuple-element.29), channel_id=1, source_target_pairs={{0,32},{1,33},{2,34},{3,35},{4,36},{5,37},{6,38},{7,39},{8,40},{9,... | collective-permute-start | bytes 983048 | tf_op jit(solution)/shard_map/ppermute | solution.py:187
  8.5 1.6 %collective-permute-start = (s32[2,32]{1,0:T(2,128)S(1)}, s32[2,32]{1,0:T(2,128)S(1)}, u32[]{:S(2)}, u32[]{:S(2)}) collective-permute-start(s32[2,32]{1,0:T(2,128)S(1)} %pad_add_fusion.left), channel_id=1, source_target_pairs={{0,1},{1,0},{2,3},{3,2},{4,5},{5,4},{6,7},{7,6},{8,9},{9,8},{10,11... | collective-permute-start | bytes 776 | tf_op jit(solution)/shard_map/ppermute | solution.py:203
  10.2 2.0 %collective-permute-done.right = s32[2,32]{1,0:T(2,128)S(1)} collective-permute-done((s32[2,32]{1,0:T(2,128)S(1)}, s32[2,32]{1,0:T(2,128)S(1)}, u32[]{:S(2)}, u32[]{:S(2)}) %collective-permute-start) | collective-permute-done | bytes 288 | tf_op jit(solution)/shard_map/ppermute | solution.py:203
  12.2 3.1 %collective-permute-start.1 = (s32[2,32]{1,0:T(2,128)S(1)}, s32[2,32]{1,0:T(2,128)S(1)}, u32[]{:S(2)}, u32[]{:S(2)}) collective-permute-start(s32[2,32]{1,0:T(2,128)S(1)} %shard_map.91.left), channel_id=1, source_target_pairs={{0,2},{1,3},{2,0},{3,1},{4,6},{5,7},{6,4},{7,5},{8,10},{9,11},{10,... | collective-permute-start | bytes 776 | tf_op jit(solution)/shard_map/ppermute | solution.py:203
  15.3 2.0 %collective-permute-done.1.right = s32[2,32]{1,0:T(2,128)S(1)} collective-permute-done((s32[2,32]{1,0:T(2,128)S(1)}, s32[2,32]{1,0:T(2,128)S(1)}, u32[]{:S(2)}, u32[]{:S(2)}) %collective-permute-start.1) | collective-permute-done | bytes 288 | tf_op jit(solution)/shard_map/ppermute | solution.py:203
  17.3 1.6 %collective-permute-start.2 = (s32[2,32]{1,0:T(2,128)S(1)}, s32[2,32]{1,0:T(2,128)S(1)}, u32[]{:S(2)}, u32[]{:S(2)}) collective-permute-start(s32[2,32]{1,0:T(2,128)S(1)} %shard_map.92.left), channel_id=1, source_target_pairs={{0,4},{1,5},{2,6},{3,7},{4,0},{5,1},{6,2},{7,3},{8,12},{9,13},{10,... | collective-permute-start | bytes 776 | tf_op jit(solution)/shard_map/ppermute | solution.py:203
  18.9 1.9 %collective-permute-done.2.right = s32[2,32]{1,0:T(2,128)S(1)} collective-permute-done((s32[2,32]{1,0:T(2,128)S(1)}, s32[2,32]{1,0:T(2,128)S(1)}, u32[]{:S(2)}, u32[]{:S(2)}) %collective-permute-start.2) | collective-permute-done | bytes 288 | tf_op jit(solution)/shard_map/ppermute | solution.py:203
  20.8 3.3 %collective-permute-start.3 = (s32[2,32]{1,0:T(2,128)S(1)}, s32[2,32]{1,0:T(2,128)S(1)}, u32[]{:S(2)}, u32[]{:S(2)}) collective-permute-start(s32[2,32]{1,0:T(2,128)S(1)} %shard_map.93.left), channel_id=1, source_target_pairs={{0,8},{1,9},{2,10},{3,11},{4,12},{5,13},{6,14},{7,15},{8,0},{9,1},... | collective-permute-start | bytes 776 | tf_op jit(solution)/shard_map/ppermute | solution.py:203
  24.1 1.8 %collective-permute-done.3.right = s32[2,32]{1,0:T(2,128)S(1)} collective-permute-done((s32[2,32]{1,0:T(2,128)S(1)}, s32[2,32]{1,0:T(2,128)S(1)}, u32[]{:S(2)}, u32[]{:S(2)}) %collective-permute-start.3) | collective-permute-done | bytes 288 | tf_op jit(solution)/shard_map/ppermute | solution.py:203
  25.9 2.0 %collective-permute-start.4 = (s32[2,32]{1,0:T(2,128)S(1)}, s32[2,32]{1,0:T(2,128)S(1)}, u32[]{:S(2)}, u32[]{:S(2)}) collective-permute-start(s32[2,32]{1,0:T(2,128)S(1)} %shard_map.94.left), channel_id=1, source_target_pairs={{0,16},{1,17},{2,18},{3,19},{4,20},{5,21},{6,22},{7,23},{8,24},{9,... | collective-permute-start | bytes 776 | tf_op jit(solution)/shard_map/ppermute | solution.py:203
  27.9 1.6 %collective-permute-done.4.right = s32[2,32]{1,0:T(2,128)S(1)} collective-permute-done((s32[2,32]{1,0:T(2,128)S(1)}, s32[2,32]{1,0:T(2,128)S(1)}, u32[]{:S(2)}, u32[]{:S(2)}) %collective-permute-start.4) | collective-permute-done | bytes 288 | tf_op jit(solution)/shard_map/ppermute | solution.py:203
  29.5 3.0 %shard_map.97 = bf16[128,1280]{1,0:T(8,128)(2,1)S(1)} custom-call(s32[3]{0:T(128)S(1)} %pad_add_fusion.1.meta.refs_0_, s32[2,32]{1,0:T(2,128)S(1)} %shard_map.95.refs_1_, f32[1,1280]{1,0:T(1,128)S(1)} %get-tuple-element.21.refs_2_, bf16[1280,2560]{1,0:T(8,128)(2,1)S(1)} %get-tuple-element.22.refs_3_, bf16[2560,1280]{1,0:T(8,128)(2,1)S(1)} %get-tuple-element.23.refs_4_, ...), custom_call_target="tpu_custom_call" | custom-call | flops 1677721600 | bytes 1048576 | tf_op jit(solution)/shard_map/pallas_call | solution.py:271
  32.5 1.3 %collective-permute-start.6 = (bf16[128,1280]{1,0:T(8,128)(2,1)S(1)}, bf16[128,1280]{1,0:T(8,128)(2,1)S(1)}, u32[]{:S(2)}, u32[]{:S(2)}) collective-permute-start(bf16[128,1280]{1,0:T(8,128)(2,1)S(1)} %shard_map.97), channel_id=1, source_target_pairs={{0,32},{1,33},{2,34},{3,35},{4,36},{5,37},{6,38},{7,39},{8,40},{9,... | collective-permute-start | bytes 983048 | tf_op jit(solution)/shard_map/ppermute | solution.py:187
  33.8 1.3 %collective-permute-start.8 = (bf16[128,1280]{1,0:T(8,128)(2,1)S(1)}, bf16[128,1280]{1,0:T(8,128)(2,1)S(1)}, u32[]{:S(2)}, u32[]{:S(2)}) collective-permute-start(bf16[128,1280]{1,0:T(8,128)(2,1)S(1)} %shard_map.97), channel_id=1, source_target_pairs={{32,64},{33,65},{34,66},{35,67},{36,68},{37,69},{38,70},{39,71},{4... | collective-permute-start | bytes 983048 | tf_op jit(solution)/shard_map/ppermute | solution.py:187
  35.1 3.0 %shard_map.98 = bf16[128,1280]{1,0:T(8,128)(2,1)S(1)} custom-call(s32[3]{0:T(128)S(1)} %pad_add_fusion.1.meta.refs_0_, s32[2,32]{1,0:T(2,128)S(1)} %shard_map.95.refs_1_, f32[1,1280]{1,0:T(1,128)S(1)} %get-tuple-element.21.refs_2_, bf16[1280,2560]{1,0:T(8,128)(2,1)S(1)} %get-tuple-element.22.refs_3_, bf16[2560,1280]{1,0:T(8,128)(2,1)S(1)} %get-tuple-element.23.refs_4_, ...), custom_call_target="tpu_custom_call" | custom-call | flops 1677721600 | bytes 1048576 | tf_op jit(solution)/shard_map/pallas_call | solution.py:271
  38.1 2.0 %collective-permute-start.7 = (bf16[128,1280]{1,0:T(8,128)(2,1)S(1)}, bf16[128,1280]{1,0:T(8,128)(2,1)S(1)}, u32[]{:S(2)}, u32[]{:S(2)}) collective-permute-start(bf16[128,1280]{1,0:T(8,128)(2,1)S(1)} %shard_map.98), channel_id=1, source_target_pairs={{0,32},{1,33},{2,34},{3,35},{4,36},{5,37},{6,38},{7,39},{8,40},{9,... | collective-permute-start | bytes 983048 | tf_op jit(solution)/shard_map/ppermute | solution.py:187
  40.2 1.3 %collective-permute-start.11 = (bf16[128,1280]{1,0:T(8,128)(2,1)S(1)}, bf16[128,1280]{1,0:T(8,128)(2,1)S(1)}, u32[]{:S(2)}, u32[]{:S(2)}) collective-permute-start(bf16[128,1280]{1,0:T(8,128)(2,1)S(1)} %get-tuple-element.29), channel_id=1, source_target_pairs={{0,96},{1,97},{2,98},{3,99},{4,100},{5,101},{6,102},{7,103},{8,104... | collective-permute-start | bytes 983048 | tf_op jit(solution)/shard_map/ppermute | solution.py:187
  43.1 3.2 %shard_map.99 = bf16[128,1280]{1,0:T(8,128)(2,1)S(1)} custom-call(s32[3]{0:T(128)S(1)} %pad_add_fusion.1.meta.refs_0_, s32[2,32]{1,0:T(2,128)S(1)} %shard_map.95.refs_1_, f32[1,1280]{1,0:T(1,128)S(1)} %get-tuple-element.21.refs_2_, bf16[1280,2560]{1,0:T(8,128)(2,1)S(1)} %get-tuple-element.22.refs_3_, bf16[2560,1280]{1,0:T(8,128)(2,1)S(1)} %get-tuple-element.23.refs_4_, ...), custom_call_target="tpu_custom_call" | custom-call | flops 1677721600 | bytes 1048576 | tf_op jit(solution)/shard_map/pallas_call | solution.py:271
  48.3 1.5 %collective-permute-done.11.refs_9_ = bf16[128,1280]{1,0:T(8,128)(2,1)S(1)} collective-permute-done((bf16[128,1280]{1,0:T(8,128)(2,1)S(1)}, bf16[128,1280]{1,0:T(8,128)(2,1)S(1)}, u32[]{:S(2)}, u32[]{:S(2)}) %collective-permute-start.11) | collective-permute-done | bytes 327712 | tf_op jit(solution)/shard_map/ppermute | solution.py:187
  49.8 3.5 %collective-permute-done.10.refs_8_.refs_9_ = bf16[128,1280]{1,0:T(8,128)(2,1)S(1)} collective-permute-done((bf16[128,1280]{1,0:T(8,128)(2,1)S(1)}, bf16[128,1280]{1,0:T(8,128)(2,1)S(1)}, u32[]{:S(2)}, u32[]{:S(2)}) %collective-permute-start.10) | collective-permute-done | bytes 327712 | tf_op jit(solution)/shard_map/ppermute | solution.py:187
  56.6 15.4 %collective-permute-start.17 = (bf16[128,1280]{1,0:T(8,128)(2,1)S(1)}, bf16[128,1280]{1,0:T(8,128)(2,1)S(1)}, u32[]{:S(2)}, u32[]{:S(2)}) collective-permute-start(bf16[128,1280]{1,0:T(8,128)(2,1)S(1)} %shard_map.99), channel_id=1, source_target_pairs={{0,96},{1,97},{2,98},{3,99},{4,100},{5,101},{6,102},{7,103},{8,104... | collective-permute-start | bytes 983048 | tf_op jit(solution)/shard_map/ppermute | solution.py:187
  73.3 3.3 %collective-permute-done.17.refs_8_ = bf16[128,1280]{1,0:T(8,128)(2,1)S(1)} collective-permute-done((bf16[128,1280]{1,0:T(8,128)(2,1)S(1)}, bf16[128,1280]{1,0:T(8,128)(2,1)S(1)}, u32[]{:S(2)}, u32[]{:S(2)}) %collective-permute-start.17) | collective-permute-done | bytes 327712 | tf_op jit(solution)/shard_map/ppermute | solution.py:187
  80.0 9.6 %collective-permute-done.20 = bf16[6,8,256]{2,1,0:T(8,128)(2,1)S(1)} collective-permute-done((bf16[6,8,256]{2,1,0:T(8,128)(2,1)S(1)}, bf16[6,8,256]{2,1,0:T(8,128)(2,1)S(1)}, u32[]{:S(2)}, u32[]{:S(2)}) %collective-permute-start.20) | collective-permute-done | bytes 24608 | tf_op jit(solution)/shard_map/ppermute | solution.py:187
  (39 shorter events, 12.5 us)
Async XLA Ops:
  0.1 8.2 %copy-start = (s32[2,2]{1,0:T(2,128)S(1)}, s32[2,2]{1,0:T(2,128)}, u32[]{:S(2)}) copy-start(s32[2,2]{1,0:T(2,128)} %param.10) | copy-start | bytes 52
  6.9 22.6 %collective-permute-start.5 = (bf16[128,1280]{1,0:T(8,128)(2,1)S(1)}, bf16[128,1280]{1,0:T(8,128)(2,1)S(1)}, u32[]{:S(2)}, u32[]{:S(2)}) collective-permute-start(bf16[128,1280]{1,0:T(8,128)(2,1)S(1)} %get-tuple-element.29), channel_id=1, source_target_pairs={{0,32},{1,33},{2,34},{3,35},{4,36},{5,37},{6,38},{7,39},{8,40},{9,... | collective-permute-start | bytes 983048 | tf_op jit(solution)/shard_map/ppermute | solution.py:187
  8.5 3.6 %collective-permute-start = (s32[2,32]{1,0:T(2,128)S(1)}, s32[2,32]{1,0:T(2,128)S(1)}, u32[]{:S(2)}, u32[]{:S(2)}) collective-permute-start(s32[2,32]{1,0:T(2,128)S(1)} %pad_add_fusion.left), channel_id=1, source_target_pairs={{0,1},{1,0},{2,3},{3,2},{4,5},{5,4},{6,7},{7,6},{8,9},{9,8},{10,11... | collective-permute-start | bytes 776 | tf_op jit(solution)/shard_map/ppermute | solution.py:203
  12.2 5.1 %collective-permute-start.1 = (s32[2,32]{1,0:T(2,128)S(1)}, s32[2,32]{1,0:T(2,128)S(1)}, u32[]{:S(2)}, u32[]{:S(2)}) collective-permute-start(s32[2,32]{1,0:T(2,128)S(1)} %shard_map.91.left), channel_id=1, source_target_pairs={{0,2},{1,3},{2,0},{3,1},{4,6},{5,7},{6,4},{7,5},{8,10},{9,11},{10,... | collective-permute-start | bytes 776 | tf_op jit(solution)/shard_map/ppermute | solution.py:203
  17.3 3.6 %collective-permute-start.2 = (s32[2,32]{1,0:T(2,128)S(1)}, s32[2,32]{1,0:T(2,128)S(1)}, u32[]{:S(2)}, u32[]{:S(2)}) collective-permute-start(s32[2,32]{1,0:T(2,128)S(1)} %shard_map.92.left), channel_id=1, source_target_pairs={{0,4},{1,5},{2,6},{3,7},{4,0},{5,1},{6,2},{7,3},{8,12},{9,13},{10,... | collective-permute-start | bytes 776 | tf_op jit(solution)/shard_map/ppermute | solution.py:203
  20.8 5.1 %collective-permute-start.3 = (s32[2,32]{1,0:T(2,128)S(1)}, s32[2,32]{1,0:T(2,128)S(1)}, u32[]{:S(2)}, u32[]{:S(2)}) collective-permute-start(s32[2,32]{1,0:T(2,128)S(1)} %shard_map.93.left), channel_id=1, source_target_pairs={{0,8},{1,9},{2,10},{3,11},{4,12},{5,13},{6,14},{7,15},{8,0},{9,1},... | collective-permute-start | bytes 776 | tf_op jit(solution)/shard_map/ppermute | solution.py:203
  25.9 3.6 %collective-permute-start.4 = (s32[2,32]{1,0:T(2,128)S(1)}, s32[2,32]{1,0:T(2,128)S(1)}, u32[]{:S(2)}, u32[]{:S(2)}) collective-permute-start(s32[2,32]{1,0:T(2,128)S(1)} %shard_map.94.left), channel_id=1, source_target_pairs={{0,16},{1,17},{2,18},{3,19},{4,20},{5,21},{6,22},{7,23},{8,24},{9,... | collective-permute-start | bytes 776 | tf_op jit(solution)/shard_map/ppermute | solution.py:203
  32.5 2.6 %collective-permute-start.6 = (bf16[128,1280]{1,0:T(8,128)(2,1)S(1)}, bf16[128,1280]{1,0:T(8,128)(2,1)S(1)}, u32[]{:S(2)}, u32[]{:S(2)}) collective-permute-start(bf16[128,1280]{1,0:T(8,128)(2,1)S(1)} %shard_map.97), channel_id=1, source_target_pairs={{0,32},{1,33},{2,34},{3,35},{4,36},{5,37},{6,38},{7,39},{8,40},{9,... | collective-permute-start | bytes 983048 | tf_op jit(solution)/shard_map/ppermute | solution.py:187
  33.8 9.3 %collective-permute-start.8 = (bf16[128,1280]{1,0:T(8,128)(2,1)S(1)}, bf16[128,1280]{1,0:T(8,128)(2,1)S(1)}, u32[]{:S(2)}, u32[]{:S(2)}) collective-permute-start(bf16[128,1280]{1,0:T(8,128)(2,1)S(1)} %shard_map.97), channel_id=1, source_target_pairs={{32,64},{33,65},{34,66},{35,67},{36,68},{37,69},{38,70},{39,71},{4... | collective-permute-start | bytes 983048 | tf_op jit(solution)/shard_map/ppermute | solution.py:187
  38.1 5.0 %collective-permute-start.7 = (bf16[128,1280]{1,0:T(8,128)(2,1)S(1)}, bf16[128,1280]{1,0:T(8,128)(2,1)S(1)}, u32[]{:S(2)}, u32[]{:S(2)}) collective-permute-start(bf16[128,1280]{1,0:T(8,128)(2,1)S(1)} %shard_map.98), channel_id=1, source_target_pairs={{0,32},{1,33},{2,34},{3,35},{4,36},{5,37},{6,38},{7,39},{8,40},{9,... | collective-permute-start | bytes 983048 | tf_op jit(solution)/shard_map/ppermute | solution.py:187
  40.2 9.7 %collective-permute-start.11 = (bf16[128,1280]{1,0:T(8,128)(2,1)S(1)}, bf16[128,1280]{1,0:T(8,128)(2,1)S(1)}, u32[]{:S(2)}, u32[]{:S(2)}) collective-permute-start(bf16[128,1280]{1,0:T(8,128)(2,1)S(1)} %get-tuple-element.29), channel_id=1, source_target_pairs={{0,96},{1,97},{2,98},{3,99},{4,100},{5,101},{6,102},{7,103},{8,104... | collective-permute-start | bytes 983048 | tf_op jit(solution)/shard_map/ppermute | solution.py:187
  41.5 11.9 %collective-permute-start.10 = (bf16[128,1280]{1,0:T(8,128)(2,1)S(1)}, bf16[128,1280]{1,0:T(8,128)(2,1)S(1)}, u32[]{:S(2)}, u32[]{:S(2)}) collective-permute-start(bf16[128,1280]{1,0:T(8,128)(2,1)S(1)} %shard_map.98), channel_id=1, source_target_pairs={{32,64},{33,65},{34,66},{35,67},{36,68},{37,69},{38,70},{39,71},{4... | collective-permute-start | bytes 983048 | tf_op jit(solution)/shard_map/ppermute | solution.py:187
  46.3 7.1 %collective-permute-start.9 = (bf16[128,1280]{1,0:T(8,128)(2,1)S(1)}, bf16[128,1280]{1,0:T(8,128)(2,1)S(1)}, u32[]{:S(2)}, u32[]{:S(2)}) collective-permute-start(bf16[128,1280]{1,0:T(8,128)(2,1)S(1)} %shard_map.99), channel_id=1, source_target_pairs={{0,32},{1,33},{2,34},{3,35},{4,36},{5,37},{6,38},{7,39},{8,40},{9,... | collective-permute-start | bytes 983048 | tf_op jit(solution)/shard_map/ppermute | solution.py:187
  47.6 7.7 %collective-permute-start.13 = (bf16[128,1280]{1,0:T(8,128)(2,1)S(1)}, bf16[128,1280]{1,0:T(8,128)(2,1)S(1)}, u32[]{:S(2)}, u32[]{:S(2)}) collective-permute-start(bf16[128,1280]{1,0:T(8,128)(2,1)S(1)} %shard_map.99), channel_id=1, source_target_pairs={{32,64},{33,65},{34,66},{35,67},{36,68},{37,69},{38,70},{39,71},{4... | collective-permute-start | bytes 983048 | tf_op jit(solution)/shard_map/ppermute | solution.py:187
  53.9 1.4 %collective-permute-start.12 = (bf16[128,1280]{1,0:T(8,128)(2,1)S(1)}, bf16[128,1280]{1,0:T(8,128)(2,1)S(1)}, u32[]{:S(2)}, u32[]{:S(2)}) collective-permute-start(bf16[128,1280]{1,0:T(8,128)(2,1)S(1)} %get-tuple-element.30), channel_id=1, source_target_pairs={{64,96},{65,97},{66,98},{67,99},{68,100},{69,101},{70,102},{71,103... | collective-permute-start | bytes 983048 | tf_op jit(solution)/shard_map/ppermute | solution.py:187
  54.6 17.4 %collective-permute-start.15 = (bf16[128,1280]{1,0:T(8,128)(2,1)S(1)}, bf16[128,1280]{1,0:T(8,128)(2,1)S(1)}, u32[]{:S(2)}, u32[]{:S(2)}) collective-permute-start(bf16[128,1280]{1,0:T(8,128)(2,1)S(1)} %get-tuple-element.30), channel_id=1, source_target_pairs={{32,64},{33,65},{34,66},{35,67},{36,68},{37,69},{38,70},{39,71},{4... | collective-permute-start | bytes 983048 | tf_op jit(solution)/shard_map/ppermute | solution.py:187
  55.9 16.1 %collective-permute-start.14 = (bf16[128,1280]{1,0:T(8,128)(2,1)S(1)}, bf16[128,1280]{1,0:T(8,128)(2,1)S(1)}, u32[]{:S(2)}, u32[]{:S(2)}) collective-permute-start(bf16[128,1280]{1,0:T(8,128)(2,1)S(1)} %get-tuple-element.32), channel_id=1, source_target_pairs={{64,96},{65,97},{66,98},{67,99},{68,100},{69,101},{70,102},{71,103... | collective-permute-start | bytes 983048 | tf_op jit(solution)/shard_map/ppermute | solution.py:187
  56.6 19.9 %collective-permute-start.17 = (bf16[128,1280]{1,0:T(8,128)(2,1)S(1)}, bf16[128,1280]{1,0:T(8,128)(2,1)S(1)}, u32[]{:S(2)}, u32[]{:S(2)}) collective-permute-start(bf16[128,1280]{1,0:T(8,128)(2,1)S(1)} %shard_map.99), channel_id=1, source_target_pairs={{0,96},{1,97},{2,98},{3,99},{4,100},{5,101},{6,102},{7,103},{8,104... | collective-permute-start | bytes 983048 | tf_op jit(solution)/shard_map/ppermute | solution.py:187
  72.6 4.0 %collective-permute-start.16 = (bf16[128,1280]{1,0:T(8,128)(2,1)S(1)}, bf16[128,1280]{1,0:T(8,128)(2,1)S(1)}, u32[]{:S(2)}, u32[]{:S(2)}) collective-permute-start(bf16[128,1280]{1,0:T(8,128)(2,1)S(1)} %get-tuple-element.34), channel_id=1, source_target_pairs={{64,96},{65,97},{66,98},{67,99},{68,100},{69,101},{70,102},{71,103... | collective-permute-start | bytes 983048 | tf_op jit(solution)/shard_map/ppermute | solution.py:187
  77.4 2.7 %collective-permute-start.18 = (bf16[6,8,256]{2,1,0:T(8,128)(2,1)S(1)}, bf16[6,8,256]{2,1,0:T(8,128)(2,1)S(1)}, u32[]{:S(2)}, u32[]{:S(2)}) collective-permute-start(bf16[6,8,256]{2,1,0:T(8,128)(2,1)S(1)} %get-tuple-element.43), channel_id=1, source_target_pairs={{96,64},{97,65},{98,66},{99,67},{100,68},{101,69},{102,70},{103,71... | collective-permute-start | bytes 73736 | tf_op jit(solution)/shard_map/ppermute | solution.py:187
  78.0 2.0 %collective-permute-start.19 = (bf16[6,8,256]{2,1,0:T(8,128)(2,1)S(1)}, bf16[6,8,256]{2,1,0:T(8,128)(2,1)S(1)}, u32[]{:S(2)}, u32[]{:S(2)}) collective-permute-start(bf16[6,8,256]{2,1,0:T(8,128)(2,1)S(1)} %get-tuple-element.42), channel_id=1, source_target_pairs={{96,32},{97,33},{98,34},{99,35},{100,36},{101,37},{102,38},{103,39... | collective-permute-start | bytes 73736 | tf_op jit(solution)/shard_map/ppermute | solution.py:187
  78.7 10.9 %collective-permute-start.20 = (bf16[6,8,256]{2,1,0:T(8,128)(2,1)S(1)}, bf16[6,8,256]{2,1,0:T(8,128)(2,1)S(1)}, u32[]{:S(2)}, u32[]{:S(2)}) collective-permute-start(bf16[6,8,256]{2,1,0:T(8,128)(2,1)S(1)} %get-tuple-element.41), channel_id=1, source_target_pairs={{96,0},{97,1},{98,2},{99,3},{100,4},{101,5},{102,6},{103,7},{104,8... | collective-permute-start | bytes 73736 | tf_op jit(solution)/shard_map/ppermute | solution.py:187
